TPU v7x, 128 devices: a whole 4x4x4 slice. The times are simulated.
128 devices in a mesh: aux: 4 (over z_lo, core), bas: 32 (over x, z_hi, y).
Axes of the slice: x: 4, y: 4, z: 4 (z_hi: 2, z_lo: 2; z = z_hi * 2 + z_lo), core: 2. Of those that a mesh axis runs over, the one named last changes fastest.
Arguments:
- slabs: bfloat16 [512, 8, 12288], P('aux', None, 'bas'), may hold values from -0.09375 to 0.09375
Outputs:
- exchange: float32 [12288, 12288], P('aux', 'bas')
All inputs are finite; a program needn't handle non-finite values.
Results may differ from a plain program's by a relative error of at most 0.0003.
Values may be sent and summed in bfloat16 or wider, within the bound.
A program may use at most 128 MiB of HBM per device.

v0:
```python
import jax
import jax.numpy as jnp
from jax import lax
from jax.sharding import PartitionSpec as P


def contract(columns, local_rows):
    return lax.dot_general(
        columns, local_rows, (((0,), (0,)), ((), ())), preferred_element_type=jnp.float32
    )


def shards(slabs):
    block_width = slabs.shape[2]
    local_rows = slabs.reshape(-1, block_width)
    piece = lax.all_gather(slabs, "bas", axis=2, tiled=True)
    partial_tiles = contract(piece.reshape(-1, piece.shape[2]), local_rows)
    return lax.psum_scatter(partial_tiles, "aux", scatter_dimension=0, tiled=True)


def solution(mesh):
    placed = (P("aux", None, "bas"),)
    return jax.shard_map(
        shards, mesh=mesh, in_specs=placed, out_specs=P("aux", "bas"), check_vma=False
    )
```

profile of v0, /device:TPU:7, one launch (start us, length us, event | category | flops | bytes accessed | tf_op | source)
XLA Modules:
  0.0 411.8 jit_solution(5457626006233148407)
XLA Ops:
  6.5 0.0 all-gather.2.cloned.1.call-start
  6.5 2.4 copy.2
  8.9 0.0 all-gather.2.cloned.1.call-update
  9.0 0.0 reduce-scatter.2.cloned.1.call-start
  9.0 212.1 %all-gather.2.cloned.1.call-done = bf16[128,8,12288]{0,2,1:T(8,128)(2,1)} async-done(((bf16[128,8,384]{0,2,1:T(8,128)(2,1)}), bf16[128,8,12288]{0,2,1:T(8,128)(2,1)}) %all-gather.2.cloned.1.call-update) | async-done | bytes 25165840 | tf_op jit(solution)/shard_map/all_gather | solution.py:16
  221.1 21.9 %convolution_bitcast_fusion = f32[12288,384]{1,0:T(8,128)} fusion(bf16[128,8,12288]{0,2,1:T(8,128)(2,1)} %all-gather.2.cloned.1.call-done, bf16[128,8,384]{0,2,1:T(8,128)(2,1)} %copy.2), kind=kOutput, calls=%fused_computation | convolution fusion | flops 9663676416 | bytes 44826624 | tf_op jit(solution)/shard_map/dot_general | solution.py:8
  243.0 0.0 reduce-scatter.2.cloned.1.call-update
  243.0 161.9 %reduce-scatter.2.cloned.1.call-done = f32[3072,384]{1,0:T(8,128)} async-done(((f32[12288,384]{1,0:T(8,128)}), f32[3072,384]{1,0:T(8,128)}) %reduce-scatter.2.cloned.1.call-update) | async-done | bytes 4718608 | tf_op jit(solution)/shard_map/reduce_scatter | solution.py:18
Async XLA Ops:
  6.5 214.5 %all-gather.2.cloned.1.call-start = ((), (), s32[]{:S(2)}) async-start(), calls=%async_computation.1 | async-start | bytes 25952256 | tf_op jit(solution)/shard_map/all_gather | solution.py:16
  9.0 396.0 %reduce-scatter.2.cloned.1.call-start = ((), (), s32[]{:S(2)}) async-start(), calls=%async_computation.2 | async-start | bytes 23592960 | tf_op jit(solution)/shard_map/reduce_scatter | solution.py:18
Sparse Core Ops, SparseCore 0:
  10.3 210.6 all-gather.1
  243.1 161.7 reduce-scatter.1
where the time goes:
time: 413 us; the launch traced here: 412 us
  waiting for transfers between devices  374 us (91%)
  matrix products  21.9 us (5%)
  between operations  13.4 us (3%)
    all_gather x1, waiting for transfers between devices, shards(): piece = lax.all_gather(slabs, 'bas', axis=2, tiled=True)  212 us
    reduce_scatter x1, waiting for transfers between devices, shards(): lax.psum_scatter(partial_tiles, 'aux', scatter_dimension=0, tiled=True)  162 us
    dot_general x1, matrix products, contract(): lax.dot_general(columns, local_rows, (((0,), (0,)), ((), ())), preferred_...  21.9 us
  transfers between devices with their start and end apart: 2, of which 2 were waited for; matrix products, arithmetic and copies ran while one was open for 0% of the time, Pallas kernels for 0%

commit v1 on v0

v1 whole, which is shorter than its diff:
```python
import functools

import jax
import jax.numpy as jnp
from jax import lax
from jax.experimental import pallas as pl
from jax.experimental.pallas import tpu as pltpu
from jax.sharding import PartitionSpec as P

MESH = pl.DeviceIdType.MESH
BLOCK, HALF, QUARTER, DEPTH = 384, 192, 96, 1024


def encode(tile):
    largest = jnp.max(jnp.abs(tile), axis=(0, 1), keepdims=True)
    largest = jnp.maximum(largest, 1e-30)
    t = tile * (16384.0 / largest)
    t2 = t * t
    code = (t2 * t2) * (t2 * t) * jnp.abs(t)
    return code.astype(jnp.bfloat16), largest * (1.0 / 16384.0)


def decode(code, factor):
    code = code.astype(jnp.float32)
    root = jnp.sqrt(jnp.sqrt(jnp.sqrt(jnp.abs(code))))
    return jnp.where(code < 0, -root, root) * factor


def kernel(bt, land, factors, cb, rb, psend, precv, pown, enc, fac, ss, rs, ls, pss, prs, rss, rrs, fss, frs, own_sem):
    aux, bas = lax.axis_index("aux"), lax.axis_index("bas")
    zl, h = aux // 2, lax.rem(aux, 2)
    x, zh, y = bas // 8, lax.rem(bas // 4, 2), lax.rem(bas, 4)
    zb = lax.rem(zl + zh, 2)

    def device(x=x, y=y, zh=zh, zl=zl, h=h):
        return (zl * 2 + h, x * 8 + zh * 4 + y)

    def ring(v, step):
        return lax.rem(v + step + 4, 4)

    right, left = {"y": ring(y, 1)}, {"y": ring(y, -1)}
    front, back = {"x": ring(x, 1)}, {"x": ring(x, -1)}
    a_dev = device(zl=1 - zl)
    b_dev = device(zl=1 - zl, zh=1 - zh)
    core_dev = device(h=1 - h)

    barrier = pltpu.get_barrier_semaphore()
    greeted = [device(**d) for d in (right, left, front, back)] + [a_dev, b_dev, core_dev]
    greeted += [device(y=ring(y, 2)), device(y=ring(y, 1), zl=1 - zl), device(y=ring(y, 2), zl=1 - zl), device(y=ring(y, 3), zl=1 - zl)]
    for d in greeted:
        pl.semaphore_signal(barrier, 1, device_id=d, device_id_type=MESH)
    pl.semaphore_wait(barrier, len(greeted))

    count = [0]
    started = []

    def send(src, dst, to):
        n = count[0]
        count[0] += 1
        copy = pltpu.make_async_remote_copy(src, dst, ss.at[n], rs.at[n], device_id=to, device_id_type=MESH)
        copy.start()
        started.append(copy)
        return copy

    def local(src, dst, n):
        copy = pltpu.make_async_copy(src, dst, ls.at[n])
        copy.start()
        return copy

    def both(src, dst, plus, minus):
        return send(src, dst, device(**plus)), send(src, dst, device(**minus))

    def forward(slots, where, plus, minus):
        lo, hi = pl.ds(0, QUARTER), pl.ds(QUARTER, QUARTER)
        a = slots(ring(where, -1)).at[lo]
        b = slots(ring(where, 1)).at[hi]
        return send(a, a, device(**plus)), send(b, b, device(**minus))

    other = 1 - zb
    a1 = send(bt.at[other], cb.at[y, zl, other], a_dev)
    b1 = send(bt.at[zb], rb.at[x, zl, zh], b_dev)
    n1 = both(bt.at[zb], cb.at[y, zl, zb], right, left)
    q0 = both(bt.at[zb], rb.at[x, zl, zh], front, back)
    a2 = [send(bt.at[zb], cb.at[y, zl, zb], a_dev)]
    l0 = local(bt, cb.at[y, zl], 0)
    l1 = local(bt.at[zb], rb.at[x, zl, zh], 1)
    l0.wait()
    l1.wait()

    def n1_slot(v):
        return cb.at[v, zl, zb]

    def n0_slot(v):
        return cb.at[v, zl, other]

    def p0_slot(v):
        return cb.at[v, 1 - zl, zb]

    def q0_slot(v):
        return rb.at[v, zl, zh]

    def q1_slot(v):
        return rb.at[v, 1 - zl, 1 - zh]

    def q2_slot(v):
        return rb.at[v, 1 - zl, zh]

    a1.wait_recv()
    b1.wait_recv()
    l2 = local(p0_slot(y), q2_slot(x), 2)
    p0 = both(p0_slot(y), p0_slot(y), right, left)
    q2 = both(p0_slot(y), q2_slot(x), front, back)
    b2 = [send(p0_slot(y), q2_slot(x), b_dev)]
    for c in n1 + q0:
        c.wait_recv()
    n1f = forward(n1_slot, y, right, left)
    q0f = forward(q0_slot, x, front, back)
    a2.append(send(n1_slot(ring(y, -1)), n1_slot(ring(y, -1)), a_dev))
    a2.append(send(n1_slot(ring(y, 1)), n1_slot(ring(y, 1)), a_dev))
    n0 = both(bt.at[other], n0_slot(y), right, left)
    q1 = both(q1_slot(x), q1_slot(x), front, back)
    l2.wait()
    for c in p0 + q2:
        c.wait_recv()
    p0f = forward(p0_slot, y, right, left)
    q2f = forward(q2_slot, x, front, back)
    b2.append(send(q2_slot(ring(x, -1)), q2_slot(ring(x, -1)), b_dev))
    b2.append(send(q2_slot(ring(x, 1)), q2_slot(ring(x, 1)), b_dev))
    for c in n1f:
        c.wait_recv()
    a2.append(send(n1_slot(ring(y, 2)), n1_slot(ring(y, 2)), a_dev))
    for c in n0 + q1:
        c.wait_recv()
    n0f = forward(n0_slot, y, right, left)
    q1f = forward(q1_slot, x, front, back)
    for c in q2f:
        c.wait_recv()
    b2.append(send(q2_slot(ring(x, 2)), q2_slot(ring(x, 2)), b_dev))

    def product(xs, ys):
        total = None
        for k in range(2):
            part = lax.dot_general(
                rb[xs, k].reshape(BLOCK, DEPTH), cb[ys, k].reshape(BLOCK, DEPTH), (((1,), (1,)), ((), ())), preferred_element_type=jnp.float32
            )
            total = part if total is None else total + part
        return total

    exchanged = []

    def task(j, i, ys):
        psend[j] = product(2 * i + 1 - h, ys)
        copy = pltpu.make_async_remote_copy(psend.at[j], precv.at[j], pss.at[j], prs.at[j], device_id=core_dev, device_id_type=MESH)
        copy.start()
        exchanged.append(copy)
        pown[j] = product(2 * i + h, ys)

    finals = []

    def finish(j, i, step):
        ys = ring(y, step)
        exchanged[j].wait_recv()
        code, factor = encode(pown[j] + precv[j])
        enc[j] = code.reshape(2, HALF, BLOCK)
        fac[j] = jnp.broadcast_to(factor, (8, 128))
        owner = device(y=ys, zl=i)
        slot = y * 2 + zb
        flip = lax.rem(i + zl, 2)
        n = step * 2 + flip
        copy = pltpu.make_async_remote_copy(enc.at[j], land.at[:, slot], rss.at[n], rrs.at[n], device_id=owner, device_id_type=MESH)
        scale = pltpu.make_async_remote_copy(fac.at[j], factors.at[slot], fss.at[n], frs.at[n], device_id=owner, device_id_type=MESH)
        if step:
            copy.start()
            scale.start()
        else:

            @pl.when(flip == 1)
            def _():
                copy.start()
                scale.start()

            @pl.when(flip == 0)
            def _():
                mine = pltpu.make_async_copy(enc.at[j], land.at[:, slot], own_sem.at[0])
                mine.start()
                scale_mine = pltpu.make_async_copy(fac.at[j], factors.at[slot], own_sem.at[1])
                scale_mine.start()
                mine.wait()
                scale_mine.wait()

    i0 = x // 2
    order = [(0, 0), (0, 3), (0, 1), (1, 0), (1, 3), (1, 1), (0, 2), (1, 2)]
    for c in list(a2[:1]) + list(b2[:1]):
        c.wait_recv()
    for c in list(a2[1:3]) + list(b2[1:3]):
        c.wait_recv()
    for c in q0f + p0f + n0f + q1f:
        c.wait_recv()
    a2[3].wait_recv()
    b2[3].wait_recv()
    for j, (flip_x, step) in enumerate(order):
        i = i0 if flip_x == 0 else 1 - i0
        task(j, i, ring(y, step))
        if j:
            fx, st = order[j - 1]
            finish(j - 1, i0 if fx == 0 else 1 - i0, st)
    fx, st = order[-1]
    finish(len(order) - 1, i0 if fx == 0 else 1 - i0, st)

    for n in range(1, 8):
        copy = pltpu.make_async_remote_copy(enc.at[0], land.at[:, 0], rss.at[n], rrs.at[n], device_id=a_dev, device_id_type=MESH)
        scale = pltpu.make_async_remote_copy(fac.at[0], factors.at[0], fss.at[n], frs.at[n], device_id=a_dev, device_id_type=MESH)
        copy.wait()
        scale.wait()
    for c in exchanged + started:
        c.wait_send()


def shards(slabs):
    flat = slabs.reshape(-1, BLOCK)
    blocks = flat.T.reshape(2, HALF, DEPTH)
    anywhere = pl.BlockSpec(memory_space=pl.ANY)
    dma = pltpu.SemaphoreType.DMA
    copies = 40
    land, factors = pl.pallas_call(
        kernel,
        out_shape=(
            jax.ShapeDtypeStruct((2, 8, HALF, BLOCK), jnp.bfloat16),
            jax.ShapeDtypeStruct((8, 8, 128), jnp.float32),
        ),
        in_specs=[anywhere],
        out_specs=(anywhere, anywhere),
        scratch_shapes=[
            pltpu.VMEM((4, 2, 2, HALF, DEPTH), jnp.bfloat16),
            pltpu.VMEM((4, 2, 2, HALF, DEPTH), jnp.bfloat16),
            pltpu.VMEM((8, BLOCK, BLOCK), jnp.float32),
            pltpu.VMEM((8, BLOCK, BLOCK), jnp.float32),
            pltpu.VMEM((8, BLOCK, BLOCK), jnp.float32),
            pltpu.VMEM((8, 2, HALF, BLOCK), jnp.bfloat16),
            pltpu.VMEM((8, 8, 128), jnp.float32),
            dma((copies,)), dma((copies,)), dma((3,)),
            dma((8,)), dma((8,)), dma((8,)), dma((8,)), dma((8,)), dma((8,)), dma((2,)),
        ],
        compiler_params=pltpu.CompilerParams(collective_id=0, has_side_effects=True, vmem_limit_bytes=50 * 2**20),
        cost_estimate=pl.CostEstimate(flops=2 * 1536 * 1536 * 2048, bytes_accessed=4 * 2**20, transcendentals=0),
    )(blocks)
    factor = factors[:, 0, 0].reshape(1, 8, 1, 1)
    return decode(land, factor).reshape(8 * BLOCK, BLOCK)


def solution(mesh):
    placed = (P("aux", None, "bas"),)
    return jax.shard_map(
        shards, mesh=mesh, in_specs=placed, out_specs=P("aux", "bas"), check_vma=False
    )
```

time: 413 us -> 105 us (0.25)
  the two profiles are of different devices: /device:TPU:7 before, /device:TPU:32 now
where the time goes in v1:
time: 105 us
  Pallas kernels  97.4 us (93%)
  other arithmetic  6.3 us (6%)
  local copies, waits for them, and re-layouts  1.55 us (1%)
    pallas_call x1, Pallas kernels, shards(): pl.pallas_call(kernel, out_shape=(jax.ShapeDtypeStruct((2, 8, HALF, BLOCK...  97.4 us
    mul x1, other arithmetic, decode(): return jnp.where(code < 0, -root, root) * factor  6.3 us

profile of v1, /device:TPU:32, one launch (start us, length us, event | category | flops | bytes accessed | tf_op | source)
XLA Modules:
  0.0 105.2 jit_solution(12833999456977002869)
XLA Ops:
  0.0 1.4 %copy.3 = bf16[1024,384]{0,1:T(8,128)(2,1)S(1)} copy(bf16[1024,384]{1,0:T(8,128)(2,1)} %bitcast.6) | data formatting | bytes 1572864 | tf_op jit(solution)/shard_map/reshape | solution.py:220
  1.4 97.4 %shard_map.17 = (bf16[2,8,192,384]{3,2,1,0:T(8,128)(2,1)S(1)}, f32[8,8,128]{2,1,0:T(8,128)S(1)}) custom-call(bf16[2,192,1024]{2,1,0:T(8,128)(2,1)S(1)} %bitcast.5), custom_call_target="tpu_custom_call" | custom-call | flops 9663676416 | bytes 4194304 | tf_op jit(solution)/shard_map/pallas_call | solution.py:225
  98.8 0.1 slice_reduce_fusion
  98.9 6.3 %fusion.3 = f32[2,8,192,384]{3,2,1,0:T(8,128)} fusion(bf16[2,8,192,384]{3,2,1,0:T(8,128)(2,1)S(1)} %get-tuple-element.7, f32[8]{0:T(128)S(1)} %slice_reduce_fusion), kind=kLoop, calls=%fused_computation.6 | loop fusion | flops 7077888 | bytes 7077920 | tf_op jit(solution)/shard_map/mul | solution.py:26

commit v2 on v0

v2 whole, which is shorter than its diff:
```python
import jax
import jax.numpy as jnp
from jax import lax
from jax.experimental import pallas as pl
from jax.experimental.pallas import tpu as pltpu
from jax.sharding import PartitionSpec as P

MESH = pl.DeviceIdType.MESH
BLOCK, HALF, QUARTER, DEPTH = 384, 192, 96, 1024
TOP = 208.0


def encode(tile):
    largest = jnp.max(jnp.abs(tile), axis=1, keepdims=True)
    largest = jnp.maximum(largest, 1e-30)
    t = tile * (TOP / largest)
    t2 = t * t
    t4 = t2 * t2
    code = (t4 * t4) * (t4 * t2) * (t * jnp.abs(t))
    return code.astype(jnp.bfloat16), largest * (1.0 / TOP)


def decode(code, factor):
    code = code.astype(jnp.float32)
    root = jnp.exp2(jnp.log2(jnp.abs(code)) * (1.0 / 16.0))
    return jnp.where(code < 0, -root, root) * factor


def place():
    aux, bas = lax.axis_index("aux"), lax.axis_index("bas")
    return aux // 2, lax.rem(aux, 2), bas // 8, lax.rem(bas // 4, 2), lax.rem(bas, 4)


def ring(v, step):
    return lax.rem(v + step + 4, 4)


def is_turned(dx, dy):
    far_x, far_y = min(dx, 4 - dx), min(dy, 4 - dy)
    return far_x < far_y or far_x == far_y > 0


def kernel(bt, out, cb, rb, part, precv, enc, fac, land, factors, staged, ss, rs, ls, pss, prs, rss, rrs, fss, frs, os, outs):
    zl, h, x, zh, y = place()
    a = zl * 2 + h
    zb = lax.rem(zl + zh, 2)
    other = 1 - zb

    def device(x=x, y=y, zh=zh, zl=zl, h=h):
        return (zl * 2 + h, x * 8 + zh * 4 + y)

    right, left = {"y": ring(y, 1)}, {"y": ring(y, -1)}
    front, back = {"x": ring(x, 1)}, {"x": ring(x, -1)}
    a_dev = device(zl=1 - zl)
    b_dev = device(zl=1 - zl, zh=1 - zh)
    core_dev = device(h=1 - h)

    barrier = pltpu.get_barrier_semaphore()
    greeted = [device(**front), device(**back), b_dev, core_dev, a_dev]
    greeted += [device(y=ring(y, step), zl=z) for step in (1, 2, 3) for z in (zl, 1 - zl)]
    for d in greeted:
        pl.semaphore_signal(barrier, 1, device_id=d, device_id_type=MESH)
    alone = a == x
    for zh1 in range(2):
        for zl1 in range(2):
            same = jnp.logical_and(alone, jnp.logical_and(zh == zh1, zl == zl1))

            @pl.when(jnp.logical_not(same))
            def _():
                pl.semaphore_signal(barrier, 1, device_id=device(x=a, zh=zh1, zl=zl1, h=lax.rem(x, 2)), device_id_type=MESH)

    pl.semaphore_wait(barrier, len(greeted) + 4 - alone.astype(jnp.int32))

    started = []

    def send(src, dst, to):
        n = len(started)
        copy = pltpu.make_async_remote_copy(src, dst, ss.at[n], rs.at[n], device_id=to, device_id_type=MESH)
        copy.start()
        started.append(copy)
        return copy

    def local(src, dst, n):
        copy = pltpu.make_async_copy(src, dst, ls.at[n])
        copy.start()
        return copy

    def both(src, dst, plus, minus):
        return [send(src, dst, device(**plus)), send(src, dst, device(**minus))]

    def forward(slots, where, plus, minus, rows=HALF):
        lo, hi = pl.ds(0, rows // 2), pl.ds(rows // 2, rows // 2)
        one = slots(ring(where, -1)).at[lo]
        two = slots(ring(where, 1)).at[hi]
        return [send(one, one, device(**plus)), send(two, two, device(**minus))]

    def n1_slot(v):
        return cb.at[v, zl, zb]

    def n0_slot(v):
        return cb.at[v, zl, other]

    def p0_slot(v):
        return cb.at[v, 1 - zl, zb]

    def p1_slot(v):
        return cb.at[v, 1 - zl, other, pl.ds(0, QUARTER)]

    def a2_slot(v):
        return cb.at[v, zl, zb, pl.ds(QUARTER, QUARTER)]

    def q0_slot(v):
        return rb.at[v, zl, zh]

    def q1_slot(v):
        return rb.at[v, 1 - zl, 1 - zh]

    def q2_slot(v):
        return rb.at[v, 1 - zl, zh]

    def arrive(*copies):
        for group in copies:
            for c in group:
                c.wait_recv()

    def product(xs, ys):
        total = None
        for k in range(2):
            term = lax.dot_general(
                rb[xs, k].reshape(BLOCK, DEPTH), cb[ys, k].reshape(BLOCK, DEPTH), (((1,), (1,)), ((), ())), preferred_element_type=jnp.float32
            )
            total = term if total is None else total + term
        return total

    tasks, ends = [], []

    def task(dx, dy):
        j = len(tasks)
        xs = ring(x, dx)
        keep = lax.rem(xs, 2) == h
        ys = ring(y, dy)
        spot = (xs // 2) * 4 + ys
        part[j] = product(xs, ys)
        copy = pltpu.make_async_remote_copy(part.at[j], precv.at[spot], pss.at[j], prs.at[spot], device_id=core_dev, device_id_type=MESH)
        pl.when(jnp.logical_not(keep))(copy.start)
        ends.append((jnp.logical_not(keep), [copy.wait_send]))
        tasks.append((dx, dy, xs, ys, keep, spot, copy))
        if j:
            finish(j - 1)

    def finish(j):
        dx, dy, xs, ys, keep, spot, exchanged = tasks[j]

        def deliver(zh1, owner, slot_zh, slot_y, mine):
            n = j * 2 + zh1
            piece = (slot_zh * 4 + slot_y) * 2 + zb
            src, src_factor = enc.at[spot, zh1], fac.at[spot, zh1]
            dst, dst_factor = land.at[slot_zh, slot_y, zb], factors.at[slot_zh, slot_y, zb]
            away = [
                pltpu.make_async_remote_copy(src, dst, rss.at[n], rrs.at[piece], device_id=owner, device_id_type=MESH),
                pltpu.make_async_remote_copy(src_factor, dst_factor, fss.at[n], frs.at[piece], device_id=owner, device_id_type=MESH),
            ]
            home = []
            if mine is not None:
                home = [pltpu.make_async_copy(src, dst, os.at[0]), pltpu.make_async_copy(src_factor, dst_factor, os.at[1])]
            ends.append((keep if mine is None else jnp.logical_and(keep, jnp.logical_not(mine)), [c.wait_send for c in away]))
            return away, home, mine

        pieces = []
        for zh1 in range(2):
            if is_turned(dx, dy):
                mine = jnp.logical_and(alone, zh == zh1) if dx == 0 else None
                pieces.append(deliver(zh1, device(x=xs, zh=zh1, zl=x // 2, h=lax.rem(x, 2)), zh, ys, mine))
            else:
                mine = xs == a if dy == 0 else None
                pieces.append(deliver(zh1, device(y=ys, zl=xs // 2), zh1, y, mine))

        @pl.when(keep)
        def _():
            exchanged.wait_recv()
            code, factor = encode((part[j] + precv[spot]).reshape(2, HALF, BLOCK))
            enc[spot] = code
            fac[spot] = jnp.broadcast_to(factor, (2, 8, BLOCK))
            for away, home, mine in pieces:
                if mine is None:
                    for c in away:
                        c.start()
                    continue

                @pl.when(jnp.logical_not(mine))
                def _():
                    for c in away:
                        c.start()

                @pl.when(mine)
                def _():
                    for c in home:
                        c.start()
                    for c in home:
                        c.wait()

    a1 = [send(bt.at[other], cb.at[y, zl, other], a_dev)]
    b1 = [send(bt.at[zb], rb.at[x, zl, zh], b_dev)]
    n1 = both(bt.at[zb], cb.at[y, zl, zb], right, left)
    q0 = both(bt.at[zb], rb.at[x, zl, zh], front, back)
    a1b = [send(bt.at[zb, pl.ds(0, QUARTER)], cb.at[y, zl, zb, pl.ds(0, QUARTER)], a_dev)]
    a2 = {0: [send(bt.at[zb, pl.ds(QUARTER, QUARTER)], a2_slot(y), a_dev)]}
    b2 = {}
    l0 = local(bt, cb.at[y, zl], 0)
    l1 = local(bt.at[zb], rb.at[x, zl, zh], 1)

    arrive(a1)
    l2 = local(p0_slot(y), q2_slot(x), 2)
    p0 = both(p0_slot(y), p0_slot(y), right, left)
    q2 = both(p0_slot(y), q2_slot(x), front, back)
    b2[0] = [send(p0_slot(y), q2_slot(x), b_dev)]
    arrive(n1)
    n1f = forward(n1_slot, y, right, left)
    for step in (3, 1):
        a2[step] = [send(a2_slot(ring(y, step)), a2_slot(ring(y, step)), a_dev)]
    arrive(q0)
    q0f = forward(q0_slot, x, front, back)
    arrive(b1)
    q1 = both(q1_slot(x), q1_slot(x), front, back)
    arrive(a1b)
    p1 = both(p1_slot(y), p1_slot(y), right, left)
    n0 = both(bt.at[other], n0_slot(y), right, left)
    arrive(q2)
    q2f = forward(q2_slot, x, front, back)
    for step in (3, 1):
        b2[step] = [send(q2_slot(ring(x, step)), q2_slot(ring(x, step)), b_dev)]
    arrive(p0)
    p0f = forward(p0_slot, y, right, left)
    arrive(n1f)
    a2[2] = [send(a2_slot(ring(y, 2)), a2_slot(ring(y, 2)), a_dev)]
    l0.wait()
    l1.wait()
    l2.wait()
    arrive(a2[0], b2[0])
    task(0, 0)
    arrive(p1)
    p1f = forward(p1_slot, y, right, left, QUARTER)
    arrive(q2f)
    b2[2] = [send(q2_slot(ring(x, 2)), q2_slot(ring(x, 2)), b_dev)]
    arrive(q1)
    q1f = forward(q1_slot, x, front, back)
    arrive(n0)
    n0f = forward(n0_slot, y, right, left)
    arrive(b2[3])
    task(3, 0)
    arrive(a2[3])
    task(0, 3)
    task(3, 3)
    arrive(b2[1])
    task(1, 0)
    task(1, 3)
    arrive(a2[1])
    task(0, 1)
    task(3, 1)
    task(1, 1)
    arrive(q0f, q1f, b2[2])
    task(2, 0)
    task(2, 3)
    task(2, 1)
    arrive(p0f, n0f, p1f, a2[2])
    task(2, 2)
    task(3, 2)
    task(1, 2)
    task(0, 2)
    finish(15)

    def unpack(k, carry):
        q = k // 2
        slot_zh = lax.rem(k, 2)
        step = q + (q == 2).astype(jnp.int32) - (q == 3).astype(jnp.int32)
        slot_y = ring(y, step)
        for slot_zb in range(2):
            mine = jnp.logical_and(slot_zb == zb, jnp.logical_or(step == 0, jnp.logical_and(alone, slot_zh == zh)))
            piece = (slot_zh * 4 + slot_y) * 2 + slot_zb

            @pl.when(jnp.logical_not(mine))
            def _():
                dst, dst_factor = land.at[slot_zh, slot_y, slot_zb], factors.at[slot_zh, slot_y, slot_zb]
                pltpu.make_async_remote_copy(enc.at[0, 0], dst, rss.at[0], rrs.at[piece], device_id=a_dev, device_id_type=MESH).wait_recv()
                pltpu.make_async_remote_copy(fac.at[0, 0], dst_factor, fss.at[0], frs.at[piece], device_id=a_dev, device_id_type=MESH).wait_recv()

        values = decode(land[slot_zh, slot_y], factors[slot_zh, slot_y, :, :1]).reshape(BLOCK, BLOCK)
        dx, dy = ring(a, -x), lax.rem(4 - step, 4)
        far_x, far_y = jnp.minimum(dx, 4 - dx), jnp.minimum(dy, 4 - dy)
        turned = jnp.logical_or(far_x < far_y, jnp.logical_and(far_x == far_y, far_x > 0))

        @pl.when(turned)
        def _():
            staged[k] = values.T

        @pl.when(jnp.logical_not(turned))
        def _():
            staged[k] = values

        rows = pl.ds(pl.multiple_of((slot_zh * 4 + slot_y) * BLOCK, BLOCK), BLOCK)
        pltpu.make_async_copy(staged.at[k], out.at[rows], outs.at[k]).start()
        return carry

    lax.fori_loop(0, 8, unpack, 0)
    for k in range(8):
        pltpu.make_async_copy(staged.at[k], out.at[pl.ds(0, BLOCK)], outs.at[k]).wait()
    for c in started:
        c.wait_send()
    for condition, waits in ends:

        @pl.when(condition)
        def _():
            for w in waits:
                w()


def shards(slabs):
    flat = slabs.reshape(-1, BLOCK)
    blocks = flat.T.reshape(2, HALF, DEPTH)
    anywhere = pl.BlockSpec(memory_space=pl.ANY)
    dma = pltpu.SemaphoreType.DMA
    copies = 43
    return pl.pallas_call(
        kernel,
        out_shape=jax.ShapeDtypeStruct((8 * BLOCK, BLOCK), jnp.float32),
        in_specs=[anywhere],
        out_specs=anywhere,
        scratch_shapes=[
            pltpu.VMEM((4, 2, 2, HALF, DEPTH), jnp.bfloat16),
            pltpu.VMEM((4, 2, 2, HALF, DEPTH), jnp.bfloat16),
            pltpu.VMEM((16, BLOCK, BLOCK), jnp.float32),
            pltpu.VMEM((8, BLOCK, BLOCK), jnp.float32),
            pltpu.VMEM((8, 2, HALF, BLOCK), jnp.bfloat16),
            pltpu.VMEM((8, 2, 8, BLOCK), jnp.float32),
            pltpu.VMEM((2, 4, 2, HALF, BLOCK), jnp.bfloat16),
            pltpu.VMEM((2, 4, 2, 8, BLOCK), jnp.float32),
            pltpu.VMEM((8, BLOCK, BLOCK), jnp.float32),
            dma((copies,)), dma((copies,)), dma((3,)),
            dma((16,)), dma((8,)), dma((32,)), dma((16,)), dma((32,)), dma((16,)), dma((2,)), dma((8,)),
        ],
        compiler_params=pltpu.CompilerParams(collective_id=0, has_side_effects=True, vmem_limit_bytes=44 * 2**20),
        cost_estimate=pl.CostEstimate(flops=2 * 1536 * 1536 * 2048, bytes_accessed=4 * 2**20, transcendentals=0),
    )(blocks)


def solution(mesh):
    placed = (P("aux", None, "bas"),)
    return jax.shard_map(
        shards, mesh=mesh, in_specs=placed, out_specs=P("aux", "bas"), check_vma=False
    )
```

time: 413 us -> 92.3 us (0.22)
  waiting for transfers between devices: 374 us -> 0 us
  Pallas kernels: 0 us -> 88.5 us
  matrix products: 21.9 us -> 0 us
  between operations: 13.4 us -> 0.02 us
    all_gather x1 -> x0, waiting for transfers between devices: 212 us -> none  [shards(): piece = lax.all_gather(slabs, 'bas', axis=2, tiled=True)]
    reduce_scatter x1 -> x0, waiting for transfers between devices: 162 us -> none  [shards(): lax.psum_scatter(partial_tiles, 'aux', scatter_dimension=0, tiled=True)]
    pallas_call x0 -> x1, Pallas kernels: none -> 88.5 us  [shards(): pl.pallas_call(kernel, out_shape=jax.ShapeDtypeStruct((8 * BLOCK, BLOCK),...]
    dot_general x1 -> x0, matrix products: 21.9 us -> none  [contract(): lax.dot_general(columns, local_rows, (((0,), (0,)), ((), ())), preferred_...]
  transfers between devices with their start and end apart: 2 -> 0, of which waited for: 2 -> 0; matrix products, arithmetic and copies ran while one was open for 0% -> 0% of each run, Pallas kernels for 0% -> 0%
where the time goes in v2:
time: 92.3 us; the launch traced here: 92.1 us
  Pallas kernels  88.5 us (96%)
  local copies, waits for them, and re-layouts  3.59 us (4%)
    pallas_call x1, Pallas kernels, shards(): pl.pallas_call(kernel, out_shape=jax.ShapeDtypeStruct((8 * BLOCK, BLOCK),...  88.5 us
    unnamed x1, local copies, waits for them, and re-layouts  2.19 us

profile of v2, /device:TPU:7, one launch (start us, length us, event | category | flops | bytes accessed | tf_op | source)
XLA Modules:
  0.0 92.1 jit_solution(1729110414877306324)
XLA Ops:
  0.0 1.4 %copy.2 = bf16[1024,384]{0,1:T(8,128)(2,1)S(1)} copy(bf16[1024,384]{1,0:T(8,128)(2,1)} %bitcast.5) | data formatting | bytes 1572864 | tf_op jit(solution)/shard_map/reshape | solution.py:318
  1.4 88.5 %shard_map.17 = f32[3072,384]{1,0:T(8,128)S(1)} custom-call(bf16[2,192,1024]{2,1,0:T(8,128)(2,1)S(1)} %bitcast.4), custom_call_target="tpu_custom_call" | custom-call | flops 9663676416 | bytes 4194304 | tf_op jit(solution)/shard_map/pallas_call | solution.py:323
  89.9 2.2 %copy.4 = f32[3072,384]{1,0:T(8,128)} copy(f32[3072,384]{1,0:T(8,128)S(1)} %shard_map.17) | data formatting | bytes 9437184

commit v3 on v2

--- a/solution.py
+++ b/solution.py
@@ -6,7 +6,7 @@
 from jax.sharding import PartitionSpec as P
 
 MESH = pl.DeviceIdType.MESH
-BLOCK, HALF, QUARTER, DEPTH = 384, 192, 96, 1024
+BLOCK, HALF, QUARTER, DEPTH = 384, 192, 128, 1024
 TOP = 208.0
 
 
@@ -35,12 +35,14 @@
     return lax.rem(v + step + 4, 4)
 
 
-def is_turned(dx, dy):
+def is_turned(dx, dy, across):
     far_x, far_y = min(dx, 4 - dx), min(dy, 4 - dy)
-    return far_x < far_y or far_x == far_y > 0
-
-
-def kernel(bt, out, cb, rb, part, precv, enc, fac, land, factors, staged, ss, rs, ls, pss, prs, rss, rrs, fss, frs, os, outs):
+    if across:
+        return (far_y == 1 and far_x != 1) or far_x == far_y == 2
+    return far_y > 0
+
+
+def kernel(block, out, bt, cb, rb, part, precv, enc, fac, land, factors, staged, ss, rs, ls, pss, prs, rss, rrs, fss, frs, os, outs):
     zl, h, x, zh, y = place()
     a = zl * 2 + h
     zb = lax.rem(zl + zh, 2)
@@ -69,6 +71,7 @@
             def _():
                 pl.semaphore_signal(barrier, 1, device_id=device(x=a, zh=zh1, zl=zl1, h=lax.rem(x, 2)), device_id_type=MESH)
 
+    bt[...] = block[...].T.reshape(2, HALF, DEPTH)
     pl.semaphore_wait(barrier, len(greeted) + 4 - alone.astype(jnp.int32))
 
     started = []
@@ -107,7 +110,7 @@
         return cb.at[v, 1 - zl, other, pl.ds(0, QUARTER)]
 
     def a2_slot(v):
-        return cb.at[v, zl, zb, pl.ds(QUARTER, QUARTER)]
+        return cb.at[v, zl, zb, pl.ds(QUARTER, HALF - QUARTER)]
 
     def q0_slot(v):
         return rb.at[v, zl, zh]
@@ -132,7 +135,7 @@
             total = term if total is None else total + term
         return total
 
-    tasks, ends = [], []
+    tasks, ends, pending, lag = [], [], [], 2
 
     def task(dx, dy):
         j = len(tasks)
@@ -145,8 +148,13 @@
         pl.when(jnp.logical_not(keep))(copy.start)
         ends.append((jnp.logical_not(keep), [copy.wait_send]))
         tasks.append((dx, dy, xs, ys, keep, spot, copy))
-        if j:
-            finish(j - 1)
+        pending.append(j)
+        if len(pending) > lag:
+            finish(pending.pop(0))
+
+    def flush():
+        while pending:
+            finish(pending.pop(0))
 
     def finish(j):
         dx, dy, xs, ys, keep, spot, exchanged = tasks[j]
@@ -167,9 +175,10 @@
             return away, home, mine
 
         pieces = []
-        for zh1 in range(2):
-            if is_turned(dx, dy):
-                mine = jnp.logical_and(alone, zh == zh1) if dx == 0 else None
+        for across in (0, 1):
+            zh1 = 1 - zh if across else zh
+            if is_turned(dx, dy, across):
+                mine = alone if dx == 0 and not across else None
                 pieces.append(deliver(zh1, device(x=xs, zh=zh1, zl=x // 2, h=lax.rem(x, 2)), zh, ys, mine))
             else:
                 mine = xs == a if dy == 0 else None
@@ -204,59 +213,57 @@
     n1 = both(bt.at[zb], cb.at[y, zl, zb], right, left)
     q0 = both(bt.at[zb], rb.at[x, zl, zh], front, back)
     a1b = [send(bt.at[zb, pl.ds(0, QUARTER)], cb.at[y, zl, zb, pl.ds(0, QUARTER)], a_dev)]
-    a2 = {0: [send(bt.at[zb, pl.ds(QUARTER, QUARTER)], a2_slot(y), a_dev)]}
+    a2 = {0: [send(bt.at[zb, pl.ds(QUARTER, HALF - QUARTER)], a2_slot(y), a_dev)]}
     b2 = {}
     l0 = local(bt, cb.at[y, zl], 0)
     l1 = local(bt.at[zb], rb.at[x, zl, zh], 1)
 
     arrive(a1)
     l2 = local(p0_slot(y), q2_slot(x), 2)
+    q2 = both(p0_slot(y), q2_slot(x), front, back)
     p0 = both(p0_slot(y), p0_slot(y), right, left)
-    q2 = both(p0_slot(y), q2_slot(x), front, back)
     b2[0] = [send(p0_slot(y), q2_slot(x), b_dev)]
+    arrive(b1)
+    q1 = both(q1_slot(x), q1_slot(x), front, back)
+    n0 = both(bt.at[other], n0_slot(y), right, left)
     arrive(n1)
-    n1f = forward(n1_slot, y, right, left)
     for step in (3, 1):
         a2[step] = [send(a2_slot(ring(y, step)), a2_slot(ring(y, step)), a_dev)]
-    arrive(q0)
-    q0f = forward(q0_slot, x, front, back)
-    arrive(b1)
-    q1 = both(q1_slot(x), q1_slot(x), front, back)
     arrive(a1b)
     p1 = both(p1_slot(y), p1_slot(y), right, left)
-    n0 = both(bt.at[other], n0_slot(y), right, left)
-    arrive(q2)
-    q2f = forward(q2_slot, x, front, back)
-    for step in (3, 1):
-        b2[step] = [send(q2_slot(ring(x, step)), q2_slot(ring(x, step)), b_dev)]
-    arrive(p0)
-    p0f = forward(p0_slot, y, right, left)
-    arrive(n1f)
-    a2[2] = [send(a2_slot(ring(y, 2)), a2_slot(ring(y, 2)), a_dev)]
     l0.wait()
     l1.wait()
     l2.wait()
+    arrive(q0, q2)
+    for step in (3, 1):
+        b2[step] = [send(q2_slot(ring(x, step)), q2_slot(ring(x, step)), b_dev)]
+    q2f = forward(q2_slot, x, front, back)
     arrive(a2[0], b2[0])
     task(0, 0)
+    arrive(p0)
+    n1f = forward(n1_slot, y, right, left)
+    arrive(q1)
+    q0f = forward(q0_slot, x, front, back)
+    q1f = forward(q1_slot, x, front, back)
+    arrive(b2[3])
+    task(3, 0)
+    arrive(q2f)
+    b2[2] = [send(q2_slot(ring(x, 2)), q2_slot(ring(x, 2)), b_dev)]
+    arrive(n0)
+    p0f = forward(p0_slot, y, right, left)
+    n0f = forward(n0_slot, y, right, left)
     arrive(p1)
     p1f = forward(p1_slot, y, right, left, QUARTER)
-    arrive(q2f)
-    b2[2] = [send(q2_slot(ring(x, 2)), q2_slot(ring(x, 2)), b_dev)]
-    arrive(q1)
-    q1f = forward(q1_slot, x, front, back)
-    arrive(n0)
-    n0f = forward(n0_slot, y, right, left)
-    arrive(b2[3])
-    task(3, 0)
-    arrive(a2[3])
+    arrive(a2[3], a2[1])
     task(0, 3)
+    task(0, 1)
+    arrive(n1f)
+    a2[2] = [send(a2_slot(ring(y, 2)), a2_slot(ring(y, 2)), a_dev)]
     task(3, 3)
+    task(3, 1)
     arrive(b2[1])
     task(1, 0)
     task(1, 3)
-    arrive(a2[1])
-    task(0, 1)
-    task(3, 1)
     task(1, 1)
     arrive(q0f, q1f, b2[2])
     task(2, 0)
@@ -267,7 +274,7 @@
     task(3, 2)
     task(1, 2)
     task(0, 2)
-    finish(15)
+    flush()
 
     def unpack(k, carry):
         q = k // 2
@@ -287,7 +294,9 @@
         values = decode(land[slot_zh, slot_y], factors[slot_zh, slot_y, :, :1]).reshape(BLOCK, BLOCK)
         dx, dy = ring(a, -x), lax.rem(4 - step, 4)
         far_x, far_y = jnp.minimum(dx, 4 - dx), jnp.minimum(dy, 4 - dy)
-        turned = jnp.logical_or(far_x < far_y, jnp.logical_and(far_x == far_y, far_x > 0))
+        both_far = jnp.logical_and(far_x == 2, far_y == 2)
+        spread = jnp.logical_or(jnp.logical_and(far_y == 1, far_x != 1), both_far)
+        turned = jnp.where(slot_zh == zh, far_y > 0, spread)
 
         @pl.when(turned)
         def _():
@@ -316,16 +325,16 @@
 
 def shards(slabs):
     flat = slabs.reshape(-1, BLOCK)
-    blocks = flat.T.reshape(2, HALF, DEPTH)
     anywhere = pl.BlockSpec(memory_space=pl.ANY)
     dma = pltpu.SemaphoreType.DMA
     copies = 43
     return pl.pallas_call(
         kernel,
         out_shape=jax.ShapeDtypeStruct((8 * BLOCK, BLOCK), jnp.float32),
-        in_specs=[anywhere],
+        in_specs=[pl.BlockSpec(memory_space=pltpu.VMEM)],
         out_specs=anywhere,
         scratch_shapes=[
+            pltpu.VMEM((2, HALF, DEPTH), jnp.bfloat16),
             pltpu.VMEM((4, 2, 2, HALF, DEPTH), jnp.bfloat16),
             pltpu.VMEM((4, 2, 2, HALF, DEPTH), jnp.bfloat16),
             pltpu.VMEM((16, BLOCK, BLOCK), jnp.float32),
@@ -340,7 +349,7 @@
         ],
         compiler_params=pltpu.CompilerParams(collective_id=0, has_side_effects=True, vmem_limit_bytes=44 * 2**20),
         cost_estimate=pl.CostEstimate(flops=2 * 1536 * 1536 * 2048, bytes_accessed=4 * 2**20, transcendentals=0),
-    )(blocks)
+    )(flat)
 
 
 def solution(mesh):

time: 92.3 us -> 87.8 us (0.951)
  the two profiles are of different devices: /device:TPU:7 before, /device:TPU:1 now
where the time goes in v3:
time: 87.8 us; the launch traced here: 87.6 us
  Pallas kernels  84.3 us (96%)
  local copies, waits for them, and re-layouts  3.32 us (4%)
    pallas_call x1, Pallas kernels, shards(): pl.pallas_call(kernel, out_shape=jax.ShapeDtypeStruct((8 * BLOCK, BLOCK),...  84.3 us
    unnamed x3, local copies, waits for them, and re-layouts  3.32 us

profile of v3, /device:TPU:1, one launch (start us, length us, event | category | flops | bytes accessed | tf_op | source)
XLA Modules:
  0.0 87.6 jit_solution(16705658694841864949)
XLA Ops:
  0.0 0.0 copy-start
  0.0 1.1 %copy-done = bf16[128,8,384]{2,1,0:T(8,128)(2,1)S(1)} copy-done((bf16[128,8,384]{2,1,0:T(8,128)(2,1)S(1)}, bf16[128,8,384]{2,1,0:T(8,128)(2,1)}, u32[]{:S(2)}) %copy-start) | copy-done | bytes 786456
  1.1 84.3 %shard_map.17 = f32[3072,384]{1,0:T(8,128)S(1)} custom-call(bf16[1024,384]{1,0:T(8,128)(2,1)S(1)} %bitcast.1), custom_call_target="tpu_custom_call" | custom-call | flops 9663676416 | bytes 4194304 | tf_op jit(solution)/shard_map/pallas_call | solution.py:331
  85.4 2.2 %copy.3 = f32[3072,384]{1,0:T(8,128)} copy(f32[3072,384]{1,0:T(8,128)S(1)} %shard_map.17) | data formatting | bytes 9437184
Async XLA Ops:
  0.0 1.1 %copy-start = (bf16[128,8,384]{2,1,0:T(8,128)(2,1)S(1)}, bf16[128,8,384]{2,1,0:T(8,128)(2,1)}, u32[]{:S(2)}) copy-start(bf16[128,8,384]{2,1,0:T(8,128)(2,1)} %param.1) | copy-start | bytes 2359300

commit v4 on v3

--- a/solution.py
+++ b/solution.py
@@ -7,23 +7,24 @@
 
 MESH = pl.DeviceIdType.MESH
 BLOCK, HALF, QUARTER, DEPTH = 384, 192, 128, 1024
+ROWS = 208
 TOP = 208.0
 
 
 def encode(tile):
     largest = jnp.max(jnp.abs(tile), axis=1, keepdims=True)
-    largest = jnp.maximum(largest, 1e-30)
-    t = tile * (TOP / largest)
+    factor = (jnp.maximum(largest, 1e-30) * (1.0 / TOP)).astype(jnp.bfloat16)
+    t = tile * (1.0 / factor.astype(jnp.float32))
     t2 = t * t
     t4 = t2 * t2
     code = (t4 * t4) * (t4 * t2) * (t * jnp.abs(t))
-    return code.astype(jnp.bfloat16), largest * (1.0 / TOP)
-
-
-def decode(code, factor):
-    code = code.astype(jnp.float32)
+    return code.astype(jnp.bfloat16), jnp.broadcast_to(factor, (2, ROWS - HALF, BLOCK))
+
+
+def decode(piece):
+    code = piece[:, :HALF].astype(jnp.float32)
     root = jnp.exp2(jnp.log2(jnp.abs(code)) * (1.0 / 16.0))
-    return jnp.where(code < 0, -root, root) * factor
+    return jnp.where(code < 0, -root, root) * piece[:, HALF : HALF + 1].astype(jnp.float32)
 
 
 def place():
@@ -42,7 +43,7 @@
     return far_y > 0
 
 
-def kernel(block, out, bt, cb, rb, part, precv, enc, fac, land, factors, staged, ss, rs, ls, pss, prs, rss, rrs, fss, frs, os, outs):
+def kernel(block, out, bt, cb, rb, part, precv, enc, land, staged, ss, rs, ls, pss, prs, rss, rrs, os, outs):
     zl, h, x, zh, y = place()
     a = zl * 2 + h
     zb = lax.rem(zl + zh, 2)
@@ -135,7 +136,7 @@
             total = term if total is None else total + term
         return total
 
-    tasks, ends, pending, lag = [], [], [], 2
+    tasks, ends, pending, lag = [], [], [], 1
 
     def task(dx, dy):
         j = len(tasks)
@@ -162,15 +163,13 @@
         def deliver(zh1, owner, slot_zh, slot_y, mine):
             n = j * 2 + zh1
             piece = (slot_zh * 4 + slot_y) * 2 + zb
-            src, src_factor = enc.at[spot, zh1], fac.at[spot, zh1]
-            dst, dst_factor = land.at[slot_zh, slot_y, zb], factors.at[slot_zh, slot_y, zb]
+            src, dst = enc.at[spot, zh1], land.at[slot_zh, slot_y, zb]
             away = [
                 pltpu.make_async_remote_copy(src, dst, rss.at[n], rrs.at[piece], device_id=owner, device_id_type=MESH),
-                pltpu.make_async_remote_copy(src_factor, dst_factor, fss.at[n], frs.at[piece], device_id=owner, device_id_type=MESH),
             ]
             home = []
             if mine is not None:
-                home = [pltpu.make_async_copy(src, dst, os.at[0]), pltpu.make_async_copy(src_factor, dst_factor, os.at[1])]
+                home = [pltpu.make_async_copy(src, dst, os.at[0])]
             ends.append((keep if mine is None else jnp.logical_and(keep, jnp.logical_not(mine)), [c.wait_send for c in away]))
             return away, home, mine
 
@@ -188,8 +187,8 @@
         def _():
             exchanged.wait_recv()
             code, factor = encode((part[j] + precv[spot]).reshape(2, HALF, BLOCK))
-            enc[spot] = code
-            fac[spot] = jnp.broadcast_to(factor, (2, 8, BLOCK))
+            enc[spot, :, :HALF] = code
+            enc[spot, :, HALF:] = factor
             for away, home, mine in pieces:
                 if mine is None:
                     for c in away:
@@ -287,11 +286,10 @@
 
             @pl.when(jnp.logical_not(mine))
             def _():
-                dst, dst_factor = land.at[slot_zh, slot_y, slot_zb], factors.at[slot_zh, slot_y, slot_zb]
+                dst = land.at[slot_zh, slot_y, slot_zb]
                 pltpu.make_async_remote_copy(enc.at[0, 0], dst, rss.at[0], rrs.at[piece], device_id=a_dev, device_id_type=MESH).wait_recv()
-                pltpu.make_async_remote_copy(fac.at[0, 0], dst_factor, fss.at[0], frs.at[piece], device_id=a_dev, device_id_type=MESH).wait_recv()
-
-        values = decode(land[slot_zh, slot_y], factors[slot_zh, slot_y, :, :1]).reshape(BLOCK, BLOCK)
+
+        values = decode(land[slot_zh, slot_y]).reshape(BLOCK, BLOCK)
         dx, dy = ring(a, -x), lax.rem(4 - step, 4)
         far_x, far_y = jnp.minimum(dx, 4 - dx), jnp.minimum(dy, 4 - dy)
         both_far = jnp.logical_and(far_x == 2, far_y == 2)
@@ -339,13 +337,11 @@
             pltpu.VMEM((4, 2, 2, HALF, DEPTH), jnp.bfloat16),
             pltpu.VMEM((16, BLOCK, BLOCK), jnp.float32),
             pltpu.VMEM((8, BLOCK, BLOCK), jnp.float32),
-            pltpu.VMEM((8, 2, HALF, BLOCK), jnp.bfloat16),
-            pltpu.VMEM((8, 2, 8, BLOCK), jnp.float32),
-            pltpu.VMEM((2, 4, 2, HALF, BLOCK), jnp.bfloat16),
-            pltpu.VMEM((2, 4, 2, 8, BLOCK), jnp.float32),
+            pltpu.VMEM((8, 2, ROWS, BLOCK), jnp.bfloat16),
+            pltpu.VMEM((2, 4, 2, ROWS, BLOCK), jnp.bfloat16),
             pltpu.VMEM((8, BLOCK, BLOCK), jnp.float32),
             dma((copies,)), dma((copies,)), dma((3,)),
-            dma((16,)), dma((8,)), dma((32,)), dma((16,)), dma((32,)), dma((16,)), dma((2,)), dma((8,)),
+            dma((16,)), dma((8,)), dma((32,)), dma((16,)), dma((2,)), dma((8,)),
         ],
         compiler_params=pltpu.CompilerParams(collective_id=0, has_side_effects=True, vmem_limit_bytes=44 * 2**20),
         cost_estimate=pl.CostEstimate(flops=2 * 1536 * 1536 * 2048, bytes_accessed=4 * 2**20, transcendentals=0),

time: 87.8 us -> 85.5 us (0.974)
  the two profiles are of different devices: /device:TPU:1 before, /device:TPU:7 now
where the time goes in v4:
time: 85.5 us; the launch traced here: 85.3 us
  Pallas kernels  81.9 us (96%)
  local copies, waits for them, and re-layouts  3.32 us (4%)
    pallas_call x1, Pallas kernels, shards(): pl.pallas_call(kernel, out_shape=jax.ShapeDtypeStruct((8 * BLOCK, BLOCK),...  81.9 us
    unnamed x3, local copies, waits for them, and re-layouts  3.32 us

profile of v4, /device:TPU:7, one launch (start us, length us, event | category | flops | bytes accessed | tf_op | source)
XLA Modules:
  0.0 85.3 jit_solution(9602715949322317239)
XLA Ops:
  0.0 0.0 copy-start
  0.0 1.1 %copy-done = bf16[128,8,384]{2,1,0:T(8,128)(2,1)S(1)} copy-done((bf16[128,8,384]{2,1,0:T(8,128)(2,1)S(1)}, bf16[128,8,384]{2,1,0:T(8,128)(2,1)}, u32[]{:S(2)}) %copy-start) | copy-done | bytes 786456
  1.1 81.9 %shard_map.17 = f32[3072,384]{1,0:T(8,128)S(1)} custom-call(bf16[1024,384]{1,0:T(8,128)(2,1)S(1)} %bitcast.1), custom_call_target="tpu_custom_call" | custom-call | flops 9663676416 | bytes 4194304 | tf_op jit(solution)/shard_map/pallas_call | solution.py:329
  83.1 2.2 %copy.3 = f32[3072,384]{1,0:T(8,128)} copy(f32[3072,384]{1,0:T(8,128)S(1)} %shard_map.17) | data formatting | bytes 9437184
Async XLA Ops:
  0.0 1.1 %copy-start = (bf16[128,8,384]{2,1,0:T(8,128)(2,1)S(1)}, bf16[128,8,384]{2,1,0:T(8,128)(2,1)}, u32[]{:S(2)}) copy-start(bf16[128,8,384]{2,1,0:T(8,128)(2,1)} %param.1) | copy-start | bytes 2359300

commit v5 on v4

--- a/solution.py
+++ b/solution.py
@@ -228,6 +228,7 @@
     arrive(n1)
     for step in (3, 1):
         a2[step] = [send(a2_slot(ring(y, step)), a2_slot(ring(y, step)), a_dev)]
+    n1f = forward(n1_slot, y, right, left)
     arrive(a1b)
     p1 = both(p1_slot(y), p1_slot(y), right, left)
     l0.wait()
@@ -240,7 +241,6 @@
     arrive(a2[0], b2[0])
     task(0, 0)
     arrive(p0)
-    n1f = forward(n1_slot, y, right, left)
     arrive(q1)
     q0f = forward(q0_slot, x, front, back)
     q1f = forward(q1_slot, x, front, back)

time: 85.5 us -> 89.5 us (1.047)
  Pallas kernels: 81.9 us -> 86 us
    pallas_call x1, Pallas kernels: 81.9 us -> 86 us  [shards(): pl.pallas_call(kernel, out_shape=jax.ShapeDtypeStruct((8 * BLOCK, BLOCK),...]
where the time goes in v5:
time: 89.5 us; the launch traced here: 89.3 us
  Pallas kernels  86 us (96%)
  local copies, waits for them, and re-layouts  3.32 us (4%)
    pallas_call x1, Pallas kernels, shards(): pl.pallas_call(kernel, out_shape=jax.ShapeDtypeStruct((8 * BLOCK, BLOCK),...  86 us
    unnamed x3, local copies, waits for them, and re-layouts  3.32 us

profile of v5, /device:TPU:7, one launch (start us, length us, event | category | flops | bytes accessed | tf_op | source)
XLA Modules:
  0.0 89.3 jit_solution(9507854783864850915)
XLA Ops:
  0.0 0.0 copy-start
  0.0 1.1 %copy-done = bf16[128,8,384]{2,1,0:T(8,128)(2,1)S(1)} copy-done((bf16[128,8,384]{2,1,0:T(8,128)(2,1)S(1)}, bf16[128,8,384]{2,1,0:T(8,128)(2,1)}, u32[]{:S(2)}) %copy-start) | copy-done | bytes 786456
  1.1 86.0 %shard_map.17 = f32[3072,384]{1,0:T(8,128)S(1)} custom-call(bf16[1024,384]{1,0:T(8,128)(2,1)S(1)} %bitcast.1), custom_call_target="tpu_custom_call" | custom-call | flops 9663676416 | bytes 4194304 | tf_op jit(solution)/shard_map/pallas_call | solution.py:329
  87.1 2.2 %copy.3 = f32[3072,384]{1,0:T(8,128)} copy(f32[3072,384]{1,0:T(8,128)S(1)} %shard_map.17) | data formatting | bytes 9437184
Async XLA Ops:
  0.0 1.1 %copy-start = (bf16[128,8,384]{2,1,0:T(8,128)(2,1)S(1)}, bf16[128,8,384]{2,1,0:T(8,128)(2,1)}, u32[]{:S(2)}) copy-start(bf16[128,8,384]{2,1,0:T(8,128)(2,1)} %param.1) | copy-start | bytes 2359300
